TPU v7x, 32 devices: a whole 2x2x4 slice. The times are simulated.
32 devices in a mesh: rows: 8 (over z, core), cols: 4 (over y, x).
Axes of the slice: x: 2, y: 2, z: 4, core: 2. Of those that a mesh axis runs over, the one named last changes fastest.
Arguments:
- feat_query: bfloat16 [128, 256, 2048], P('rows', 'cols'), may hold values from -30 to 30
- feat_key: bfloat16 [128, 256, 2048], P('rows', 'cols'), may hold values from -30 to 30
- w_hidden: bfloat16 [2048, 2048], replicated, may hold values from -0.125 to 0.125
- w_out: bfloat16 [2048, 256], replicated, may hold values from -0.125 to 0.125
- w_prop: bfloat16 [256, 256], replicated, may hold values from -0.375 to 0.375
- valid_mask: int32 [128, 256], P('rows', 'cols'), may hold values 0 or 1
- neg_shard: int32 [8, 4, 8, 2], P('rows', 'cols'), may hold values from 0 to 7, as said below
- neg_block: int32 [8, 4, 8, 2], P('rows', 'cols'), may hold values from 0 to 7
Outputs:
- loss_map: float32 [128, 256], P('rows', 'cols')
Inputs may be any that keep to these rules, and one draw needn't show every extreme that they name: `neg_shard`: among the 16 entries of one tile, no shard number appears more than 2 times, and some shard number appears exactly 2 times.
All inputs are finite; a program needn't handle non-finite values. No bound on the sum of `valid_mask` on one device may be relied on, other than what follows from the above.
Results may differ from a plain program's by a relative error of at most 0.0006.
Values may be sent and summed in bfloat16 or wider, within the bound.
A program may use at most 128 MiB of HBM per device.

v0:
```python
import jax
import jax.numpy as jnp
from jax import lax
from jax.sharding import PartitionSpec as P

epsilon = 1e-06
sharpness_divisor = 0.1


def from_partner(value, axis, bit):
    mask = 2**bit
    pairs = [(source, source ^ mask) for source in range(lax.axis_size(axis))]
    return lax.ppermute(value, axis, pairs)


def padded_2(array, sides, width):
    for axis, dim in sides:
        devices, length = (lax.axis_size(axis), array.shape[dim])
        up = [(i, (i + 1) % devices) for i in range(devices - 1)]
        down = [(j, i) for i, j in up]
        last = lax.slice_in_dim(array, length - width, length, axis=dim)
        leading = lax.slice_in_dim(array, 0, width, axis=dim)
        before = lax.ppermute(last, axis, up)
        after = lax.ppermute(leading, axis, down)
        array = jnp.concatenate([before, array, after], axis=dim)
    return array


def normalize(vector):
    return vector * lax.rsqrt(jnp.sum(vector * vector, axis=-1, keepdims=True) + epsilon)


def project(feat_map, w_hidden, w_out):
    height, columns, channels = feat_map.shape
    flat_rows = feat_map.reshape(height * columns, channels)
    hidden = jnp.maximum(
        jnp.dot(flat_rows, w_hidden, preferred_element_type=jnp.float32), 0.0
    ).astype(jnp.bfloat16)
    embedded = normalize(jnp.dot(hidden, w_out, preferred_element_type=jnp.float32)).astype(
        jnp.bfloat16
    )
    return embedded.reshape(height, columns, -1)


def per_device(feat_query, feat_key, w_hidden, w_out, w_prop, valid_mask, neg_shard, neg_block):
    height, columns, channels = feat_query.shape
    per_tile = height * columns // 128
    target_embedding_lattice = project(feat_key, w_hidden, w_out)
    proj_width = target_embedding_lattice.shape[-1]
    key_blocks = target_embedding_lattice.reshape(per_tile, 128, proj_width)
    bit_total = lax.axis_size("cols").bit_length() - 1
    bit_order = list(range(bit_total))
    current = target_embedding_lattice
    for bit_number in bit_order:
        current = from_partner(current, "cols", bit_number)
    partner = current[:, ::-1]
    shard_ids = neg_shard.reshape(-1)
    block_ids = neg_block.reshape(-1)
    gathered_keys = lax.all_gather(key_blocks, "rows", axis=0, tiled=True)
    contrast_pair_agreements = gathered_keys[shard_ids * per_tile + block_ids]
    contrast_pair_agreements = contrast_pair_agreements.reshape(per_tile, -1, 128, proj_width)
    query_map = project(feat_query, w_hidden, w_out)
    padded = padded_2(query_map, (("rows", 0), ("cols", 1)), 1)
    carried = jnp.dot(padded.reshape(-1, proj_width), w_prop, preferred_element_type=jnp.float32)
    carried = carried.reshape(height + 2, columns + 2, proj_width)
    spread = jnp.zeros((height, columns, proj_width), jnp.float32)
    for row_off in range(3):
        for col_off in range(3):
            beside = padded[row_off : row_off + height, col_off : col_off + columns]
            cosine = jnp.einsum(
                "hwp,hwp->hw", query_map, beside, preferred_element_type=jnp.float32
            )
            weight = jnp.maximum(cosine, 0.0) ** 2
            spread = (
                spread
                + weight[..., None]
                * carried[row_off : row_off + height, col_off : col_off + columns]
            )
    diffused_pixel_embeddings = normalize(spread).astype(jnp.bfloat16)
    matched_pair_agreement = (
        jnp.einsum(
            "hwp,hwp->hw", diffused_pixel_embeddings, partner, preferred_element_type=jnp.float32
        )
        / sharpness_divisor
    )
    query_blocks = diffused_pixel_embeddings.reshape(per_tile, 128, proj_width)
    cosine_match_energies = (
        jnp.einsum(
            "bip,bnjp->binj",
            query_blocks,
            contrast_pair_agreements,
            preferred_element_type=jnp.float32,
        )
        / sharpness_divisor
    )
    negsum = jnp.sum(jnp.exp(cosine_match_energies), axis=(2, 3)).reshape(height, columns)
    denominator = jnp.exp(matched_pair_agreement) + negsum
    return valid_mask.astype(jnp.float32) * (jnp.log(denominator) - matched_pair_agreement)


def solution(mesh):
    in_specs = (
        P("rows", "cols", None),
        P("rows", "cols", None),
        P(),
        P(),
        P(),
        P("rows", "cols"),
        P("rows", "cols", None, None),
        P("rows", "cols", None, None),
    )
    out_specs = P("rows", "cols")
    return jax.shard_map(
        per_device, mesh=mesh, in_specs=in_specs, out_specs=out_specs, check_vma=False
    )
```

profile of v0, /device:TPU:18, one launch (start us, length us, event | category | flops | bytes accessed | tf_op | source)
XLA Modules:
  0.0 86.9 jit_solution(12206049714816552792)
XLA Ops:
  6.5 0.0 copy-start
  6.5 0.0 all-gather.2.cloned.1.call-start
  6.5 1.2 %copy-done = bf16[2048,256]{1,0:T(8,128)(2,1)S(1)} copy-done((bf16[2048,256]{1,0:T(8,128)(2,1)S(1)}, bf16[2048,256]{1,0:T(8,128)(2,1)}, u32[]{:S(2)}) %copy-start) | copy-done | bytes 1048600
  7.8 14.8 %multiply_reduce_fusion = (f32[1024]{0:T(1024)S(1)}, f32[1024,256]{1,0:T(8,128)S(1)}) fusion(bf16[2048,256]{1,0:T(8,128)(2,1)S(1)} %copy-done, bf16[1024,2048]{1,0:T(8,128)(2,1)} %bitcast.38, bf16[2048,2048]{1,0:T(8,128)(2,1)} %param.10), kind=kOutput, calls=%fused_computation.46 | convolution fusion | flops 9668393984 | bytes 14684160 | tf_op jit(solution)/shard_map/dot_general | solution.py:39
  22.5 1.0 %multiply_convert_fusion = bf16[1024,256]{1,0:T(8,128)(2,1)} fusion(f32[1024,256]{1,0:T(8,128)S(1)} %get-tuple-element.28, f32[1024]{0:T(1024)S(1)} %add_rsqrt_fusion.1), kind=kLoop, calls=%fused_computation.45 | loop fusion | flops 524288 | bytes 1576960 | tf_op jit(solution)/shard_map/convert_element_type | solution.py:39
  23.5 0.0 all-gather.2.cloned.1.call-update
  23.6 0.0 copy-start.1
  23.6 0.0 copy-start.3
  23.6 0.0 copy-start.4
  23.6 15.0 %multiply_reduce_fusion.2 = (f32[1024]{0:T(1024)S(1)}, f32[1024,256]{1,0:T(8,128)S(1)}) fusion(bf16[2048,256]{1,0:T(8,128)(2,1)S(1)} %copy-done, bf16[1024,2048]{1,0:T(8,128)(2,1)} %bitcast.39, bf16[2048,2048]{1,0:T(8,128)(2,1)} %param.10), kind=kOutput, calls=%fused_computation.50 | convolution fusion | flops 9668393984 | bytes 14684160 | tf_op jit(solution)/shard_map/dot_general | solution.py:39
  38.6 0.0 copy-start.5
  38.6 0.2 multiply_convert_fusion.2
  38.8 1.9 %collective-permute-start = (bf16[1,64,256]{2,1,0:T(8,128)(2,1)S(1)}, bf16[1,64,256]{2,1,0:T(8,128)(2,1)S(1)}, u32[]{:S(2)}, u32[]{:S(2)}) collective-permute-start(bf16[1,64,256]{2,1,0:T(8,128)(2,1)S(1)} %get-tuple-element.25), channel_id=1, source_target_pairs={{0,4},{4,8},{8,12},{12,16},{16,20},{20,24},{24,28},{1,5},{5,9},{9,... | collective-permute-start | bytes 98312 | tf_op jit(solution)/shard_map/ppermute | solution.py:23
  40.8 3.6 %collective-permute-start.1 = (bf16[1,64,256]{2,1,0:T(8,128)(2,1)S(1)}, bf16[1,64,256]{2,1,0:T(8,128)(2,1)S(1)}, u32[]{:S(2)}, u32[]{:S(2)}) collective-permute-start(bf16[1,64,256]{2,1,0:T(8,128)(2,1)S(1)} %get-tuple-element.26), channel_id=1, source_target_pairs={{4,0},{8,4},{12,8},{16,12},{20,16},{24,20},{28,24},{5,1},{9,5},{13... | collective-permute-start | bytes 98312 | tf_op jit(solution)/shard_map/ppermute | solution.py:24
  44.4 0.0 copy-done.1
  44.4 0.6 collective-permute-start.4
  45.0 0.0 copy-done.3
  45.0 0.0 copy-done.4
  45.0 0.1 copy.11
  45.1 0.1 add.90
  45.2 0.0 collective-permute-done
  45.2 2.2 %collective-permute-done.1 = bf16[1,64,256]{2,1,0:T(8,128)(2,1)S(1)} collective-permute-done((bf16[1,64,256]{2,1,0:T(8,128)(2,1)S(1)}, bf16[1,64,256]{2,1,0:T(8,128)(2,1)S(1)}, u32[]{:S(2)}, u32[]{:S(2)}) %collective-permute-start.1) | collective-permute-done | bytes 32800 | tf_op jit(solution)/shard_map/ppermute | solution.py:24
  47.4 3.4 %collective-permute-start.2 = (bf16[18,1,256]{2,1,0:T(2,128)(2,1)S(1)}, bf16[18,1,256]{2,1,0:T(2,128)(2,1)S(1)}, u32[]{:S(2)}, u32[]{:S(2)}) collective-permute-start(bf16[18,1,256]{2,1,0:T(2,128)(2,1)S(1)} %get-tuple-element.23), channel_id=1, source_target_pairs={{0,1},{1,2},{2,3},{4,5},{5,6},{6,7},{8,9},{9,10},{10,11},{12,13},{... | collective-permute-start | bytes 27656 | tf_op jit(solution)/shard_map/ppermute | solution.py:23
  50.8 2.4 %collective-permute-start.3 = (bf16[18,1,256]{2,1,0:T(2,128)(2,1)S(1)}, bf16[18,1,256]{2,1,0:T(2,128)(2,1)S(1)}, u32[]{:S(2)}, u32[]{:S(2)}) collective-permute-start(bf16[18,1,256]{2,1,0:T(2,128)(2,1)S(1)} %get-tuple-element.24), channel_id=1, source_target_pairs={{1,0},{2,1},{3,2},{5,4},{6,5},{7,6},{9,8},{10,9},{11,10},{13,12},{... | collective-permute-start | bytes 27656 | tf_op jit(solution)/shard_map/ppermute | solution.py:24
  53.3 5.4 %collective-permute-done.2 = bf16[18,1,256]{2,1,0:T(2,128)(2,1)S(1)} collective-permute-done((bf16[18,1,256]{2,1,0:T(2,128)(2,1)S(1)}, bf16[18,1,256]{2,1,0:T(2,128)(2,1)S(1)}, u32[]{:S(2)}, u32[]{:S(2)}) %collective-permute-start.2) | collective-permute-done | bytes 9248 | tf_op jit(solution)/shard_map/ppermute | solution.py:23
  58.7 1.3 %collective-permute-done.3 = bf16[18,1,256]{2,1,0:T(2,128)(2,1)S(1)} collective-permute-done((bf16[18,1,256]{2,1,0:T(2,128)(2,1)S(1)}, bf16[18,1,256]{2,1,0:T(2,128)(2,1)S(1)}, u32[]{:S(2)}, u32[]{:S(2)}) %collective-permute-start.3) | collective-permute-done | bytes 9248 | tf_op jit(solution)/shard_map/ppermute | solution.py:24
  60.0 0.4 pad_maximum_fusion
  60.4 1.5 %fusion.4 = (f32[16,64]{1,0:T(8,128)S(1)}, f32[16,64]{1,0:T(8,128)S(1)}, f32[16,64]{1,0:T(8,128)S(1)}, f32[16,64]{1,0:T(8,128)S(1)}, f32[16,64]{1,0:T(8,128)S(1)...) fusion(bf16[16,64,256]{2,1,0:T(8,128)(2,1)S(1)} %bitcast.32, ...), kind=kLoop, calls=%fused_computation.17 | loop fusion | flops 7592960 | bytes 3772416 | tf_op jit(solution)/shard_map/hwp,hwp->hw/dot_general | solution.py:70
  62.0 0.0 copy-done.5
  62.0 0.4 fusion.22
  62.4 0.0 collective-permute-done.4
  62.4 0.4 collective-permute-start.5
  62.8 1.9 %multiply_reduce_fusion.1 = (f32[16,64]{1,0:T(8,128)S(1)}, f32[16,64,256]{2,1,0:T(8,128)S(1)}) fusion(f32[18,66,256]{2,1,0:T(8,128)S(1)} %fusion.22, f32[16,64]{1,0:T(8,128)S(1)} %get-tuple-element.31, f32[16,64]{1,0:T(8,128)S(1)} %get-tuple-element.32, f32[16,64]{1,0:T(8,128)S(1)} %get-tuple-element.33, f32[16,64]{1,0:T(8,128)S(1)} %get-tuple-element.34, ...), kind=kLoop, calls=%fused_computation.48 | loop fusion | flops 4979712 | bytes 10526720 | tf_op jit(solution)/shard_map/reduce_sum | solution.py:30
  64.7 0.0 copy-start.2
  64.7 10.5 %collective-permute-done.5 = bf16[16,64,256]{2,1,0:T(8,128)(2,1)S(1)} collective-permute-done((bf16[16,64,256]{2,1,0:T(8,128)(2,1)S(1)}, bf16[16,64,256]{2,1,0:T(8,128)(2,1)S(1)}, u32[]{:S(2)}, u32[]{:S(2)}) %collective-permute-start.5) | collective-permute-done | bytes 524320 | tf_op jit(solution)/shard_map/ppermute | solution.py:13
  75.3 0.4 rev.3
  75.6 0.4 fusion.21
  76.0 0.0 all-gather.2.cloned.1.call-done
  76.1 2.8 %gather_fusion = bf16[16,128,256]{2,1,0:T(8,128)(2,1)S(1)} fusion(bf16[64,128,256]{2,1,0:T(8,128)(2,1)} %all-gather.2.cloned.1.call-done, s32[1024]{0:T(1024)S(1)} %pad_clamp_fusion), kind=kCustom, calls=%fused_computation | custom fusion | bytes 2097216 | tf_op jit(solution)/shard_map/gather | solution.py:60
  78.9 0.4 fusion.1
  79.3 0.1 reshape.94
  79.4 0.0 copy-done.2
  79.4 0.6 subtract_multiply_fusion
  (13 shorter events, 0.1 us)
Async XLA Ops:
  6.5 1.2 %copy-start = (bf16[2048,256]{1,0:T(8,128)(2,1)S(1)}, bf16[2048,256]{1,0:T(8,128)(2,1)}, u32[]{:S(2)}) copy-start(bf16[2048,256]{1,0:T(8,128)(2,1)} %param.11) | copy-start | bytes 3145732
  6.5 69.5 %all-gather.2.cloned.1.call-start = ((), (), s32[]{:S(2)}) async-start(), calls=%async_computation | async-start | bytes 4718592 | tf_op jit(solution)/shard_map/all_gather | solution.py:59
  23.6 20.8 %copy-start.1 = (bf16[1024,256]{1,0:T(8,128)(2,1)S(1)}, bf16[1024,256]{1,0:T(8,128)(2,1)}, u32[]{:S(2)}) copy-start(bf16[1024,256]{1,0:T(8,128)(2,1)} %multiply_convert_fusion) | copy-start | bytes 1572868
  23.6 21.4 %copy-start.3 = (s32[1,1,8,2]{2,3,1,0:T(2,128)S(1)}, s32[1,1,8,2]{2,3,1,0:T(2,128)}, u32[]{:S(2)}) copy-start(s32[1,1,8,2]{2,3,1,0:T(2,128)} %param.15) | copy-start | bytes 196
  23.6 21.4 %copy-start.4 = (s32[1,1,8,2]{2,3,1,0:T(2,128)S(1)}, s32[1,1,8,2]{2,3,1,0:T(2,128)}, u32[]{:S(2)}) copy-start(s32[1,1,8,2]{2,3,1,0:T(2,128)} %param.14) | copy-start | bytes 196
  38.6 23.4 %copy-start.5 = (bf16[256,256]{1,0:T(8,128)(2,1)S(1)}, bf16[256,256]{1,0:T(8,128)(2,1)}, u32[]{:S(2)}) copy-start(bf16[256,256]{1,0:T(8,128)(2,1)} %param.12) | copy-start | bytes 393220
  38.8 6.4 %collective-permute-start = (bf16[1,64,256]{2,1,0:T(8,128)(2,1)S(1)}, bf16[1,64,256]{2,1,0:T(8,128)(2,1)S(1)}, u32[]{:S(2)}, u32[]{:S(2)}) collective-permute-start(bf16[1,64,256]{2,1,0:T(8,128)(2,1)S(1)} %get-tuple-element.25), channel_id=1, source_target_pairs={{0,4},{4,8},{8,12},{12,16},{16,20},{20,24},{24,28},{1,5},{5,9},{9,... | collective-permute-start | bytes 98312 | tf_op jit(solution)/shard_map/ppermute | solution.py:23
  40.8 6.6 %collective-permute-start.1 = (bf16[1,64,256]{2,1,0:T(8,128)(2,1)S(1)}, bf16[1,64,256]{2,1,0:T(8,128)(2,1)S(1)}, u32[]{:S(2)}, u32[]{:S(2)}) collective-permute-start(bf16[1,64,256]{2,1,0:T(8,128)(2,1)S(1)} %get-tuple-element.26), channel_id=1, source_target_pairs={{4,0},{8,4},{12,8},{16,12},{20,16},{24,20},{28,24},{5,1},{9,5},{13... | collective-permute-start | bytes 98312 | tf_op jit(solution)/shard_map/ppermute | solution.py:24
  44.4 18.0 %collective-permute-start.4 = (bf16[16,64,256]{2,1,0:T(8,128)(2,1)S(1)}, bf16[16,64,256]{2,1,0:T(8,128)(2,1)S(1)}, u32[]{:S(2)}, u32[]{:S(2)}) collective-permute-start(bf16[16,64,256]{2,1,0:T(8,128)(2,1)S(1)} %bitcast.35), channel_id=1, source_target_pairs={{0,1},{1,0},{2,3},{3,2},{4,5},{5,4},{6,7},{7,6},{8,9},{9,8},{10,11... | collective-permute-start | bytes 1572872 | tf_op jit(solution)/shard_map/ppermute | solution.py:13
  47.4 11.2 %collective-permute-start.2 = (bf16[18,1,256]{2,1,0:T(2,128)(2,1)S(1)}, bf16[18,1,256]{2,1,0:T(2,128)(2,1)S(1)}, u32[]{:S(2)}, u32[]{:S(2)}) collective-permute-start(bf16[18,1,256]{2,1,0:T(2,128)(2,1)S(1)} %get-tuple-element.23), channel_id=1, source_target_pairs={{0,1},{1,2},{2,3},{4,5},{5,6},{6,7},{8,9},{9,10},{10,11},{12,13},{... | collective-permute-start | bytes 27656 | tf_op jit(solution)/shard_map/ppermute | solution.py:23
  50.8 9.2 %collective-permute-start.3 = (bf16[18,1,256]{2,1,0:T(2,128)(2,1)S(1)}, bf16[18,1,256]{2,1,0:T(2,128)(2,1)S(1)}, u32[]{:S(2)}, u32[]{:S(2)}) collective-permute-start(bf16[18,1,256]{2,1,0:T(2,128)(2,1)S(1)} %get-tuple-element.24), channel_id=1, source_target_pairs={{1,0},{2,1},{3,2},{5,4},{6,5},{7,6},{9,8},{10,9},{11,10},{13,12},{... | collective-permute-start | bytes 27656 | tf_op jit(solution)/shard_map/ppermute | solution.py:24
  62.4 12.9 %collective-permute-start.5 = (bf16[16,64,256]{2,1,0:T(8,128)(2,1)S(1)}, bf16[16,64,256]{2,1,0:T(8,128)(2,1)S(1)}, u32[]{:S(2)}, u32[]{:S(2)}) collective-permute-start(bf16[16,64,256]{2,1,0:T(8,128)(2,1)S(1)} %collective-permute-done.4), channel_id=1, source_target_pairs={{0,2},{1,3},{2,0},{3,1},{4,6},{5,7},{6,4},{7,5},{8,10},{9,11},{10,... | collective-permute-start | bytes 1572872 | tf_op jit(solution)/shard_map/ppermute | solution.py:13
  64.7 14.7 %copy-start.2 = (s32[16,64]{1,0:T(8,128)S(1)}, s32[16,64]{1,0:T(8,128)}, u32[]{:S(2)}) copy-start(s32[16,64]{1,0:T(8,128)} %param.13) | copy-start | bytes 12292
Sparse Core Ops, SparseCore 0:
  23.7 47.2 all-gather.1
where the time goes:
time: 87.1 us; the launch traced here: 86.9 us
  matrix products  30.5 us (35%)
  waiting for transfers between devices  19.5 us (22%)
  between operations  13.6 us (16%)
  starting transfers between devices  12.4 us (14%)
  other arithmetic  6.11 us (7%)
  local copies, waits for them, and re-layouts  4.65 us (5%)
    dot_general x2, matrix products, project(): jnp.dot(hidden, w_out, preferred_element_type=jnp.float32)  29.7 us
    ppermute x2, waiting for transfers between devices, from_partner(): return lax.ppermute(value, axis, pairs)  10.6 us
    ppermute x2, starting transfers between devices, padded_2(): after = lax.ppermute(leading, axis, down)  6.08 us
    ppermute x2, waiting for transfers between devices, padded_2(): before = lax.ppermute(last, axis, up)  5.38 us
    ppermute x2, starting transfers between devices, padded_2(): before = lax.ppermute(last, axis, up)  5.32 us
    ppermute x2, waiting for transfers between devices, padded_2(): after = lax.ppermute(leading, axis, down)  3.52 us
    gather x1, local copies, waits for them, and re-layouts, per_device(): contrast_pair_agreements = gathered_keys[shard_ids * per_tile + block_ids]  2.8 us
    reduce_sum x1, other arithmetic, normalize(): jnp.sum(vector * vector, axis=-1, keepdims=True) + epsilon  1.87 us
  transfers between devices with their start and end apart: 7, of which 4 were waited for; matrix products, arithmetic and copies ran while one was open for 23% of the time, Pallas kernels for 0%

commit v1 on v0

v1 whole, which is shorter than its diff:
```python
import functools

import jax
import jax.numpy as jnp
from jax import lax
from jax.experimental import pallas as pl
from jax.experimental.pallas import tpu as pltpu
from jax.sharding import PartitionSpec as P

EPS = 1e-06
INV_SHARP = 10.0
CHUNK = 256
HOP_LAG = 2
GROUP = 4
BLOCK = 128
F32, BF16 = jnp.float32, jnp.bfloat16
MESH = pl.DeviceIdType.MESH


def normalize(v):
    return v * lax.rsqrt(jnp.sum(v * v, axis=-1, keepdims=True) + EPS)


def dot_t(a, b):
    return lax.dot_general(a, b, (((1,), (1,)), ((), ())), preferred_element_type=F32)


def dot_split(a, b):
    high = a.astype(BF16)
    low = (a - high.astype(F32)).astype(BF16)
    return jnp.dot(high, b, preferred_element_type=F32) + jnp.dot(
        low, b, preferred_element_type=F32
    )


def kernel(
    n_rows, n_cols,
    fq, fk, wh, wo, wp, valid, shard, block, out,
    X, WH, WO, KG, PK, PQ, CF, CB, HB, BAND, PR,
    load, load_w, zr, send_r, send_l, send_s, recv_s, part_s, part_r, halo_s, halo_r,
):
    r, c = lax.axis_index("rows"), lax.axis_index("cols")
    lane, p = lax.rem(r, 2), r // 2
    line = n_rows // 2
    sister = r + 1 - 2 * lane
    height, width = valid.shape
    pixels, per_tile = height * width, height * width // BLOCK
    n_key = pixels // CHUNK
    img = CHUNK // width
    per_chunk = CHUNK // BLOCK
    pitch = PQ.shape[1]

    loads = [pltpu.make_async_copy(wh, WH, load_w.at[0]), pltpu.make_async_copy(wo, WO, load_w.at[1])]
    for k in range(2 * n_key):
        source = fk if k < n_key else fq
        loads.append(
            pltpu.make_async_copy(
                source.at[pl.ds((k % n_key) * CHUNK, CHUNK)], X.at[k], load.at[k]
            )
        )
    for k in (2, 0, 1, *range(3, len(loads))):
        loads[k].start()

    HB[...] = jnp.zeros(HB.shape, BF16)
    PQ[...] = jnp.zeros(PQ.shape, BF16)

    span = (GROUP + 2) * pitch
    shape = (GROUP, width, span)
    a = lax.broadcasted_iota(jnp.int32, shape, 0)
    w = lax.broadcasted_iota(jnp.int32, shape, 1)
    t = lax.broadcasted_iota(jnp.int32, shape, 2)
    down = t // pitch
    j = t - down * pitch
    near = ((j < width) & (j - w <= 1) & (w - j <= 1)) | ((j == width) & (w == width - 1)) | ((j == width + 1) & (w == 0))
    near = near & (down >= a) & (down <= a + 2)
    BAND[...] = jnp.where(near, 1.0, 0.0).astype(F32).reshape(BAND.shape)

    around = [(dr, dc) for dr in (-1, 0, 1) for dc in (-1, 0, 1) if (dr, dc) != (0, 0)]

    def inside(dr, dc):
        return (r + dr >= 0) & (r + dr < n_rows) & (c + dc >= 0) & (c + dc < n_cols)

    barrier = pltpu.get_barrier_semaphore()

    def greet(target):
        pl.semaphore_signal(barrier, inc=1, device_id=target, device_id_type=MESH)

    mirrored = (r, n_cols - 1 - c)
    friends = [(True, (sister, c)), (True, mirrored), (p > 0, (r - 2, c)), (p < line - 1, (r + 2, c))]
    friends += [(inside(dr, dc), (r + dr, c + dc)) for dr, dc in around]
    for there, target in friends:
        if there is True:
            greet(target)
        else:
            pl.when(there)(functools.partial(greet, target))
    met = sum(1 if there is True else there.astype(jnp.int32) for there, _ in friends)
    pl.semaphore_wait(barrier, met)

    def keys_of(q, own, i):
        return KG.at[2 * q + own, pl.ds(i * per_chunk, per_chunk)]

    def copy_z(q, i, right):
        ref = keys_of(q, lane, i)
        return pltpu.make_async_remote_copy(
            src_ref=ref, dst_ref=ref,
            send_sem=(send_r if right else send_l).at[q, i], recv_sem=zr.at[q, i],
            device_id=(r + 2 if right else r - 2, c), device_id_type=MESH,
        )

    def copy_s(q, i, own):
        ref = keys_of(q, own, i)
        return pltpu.make_async_remote_copy(
            src_ref=ref, dst_ref=ref,
            send_sem=send_s.at[q, i], recv_sem=recv_s.at[q, i],
            device_id=(sister, c), device_id_type=MESH,
        )

    def copy_p(i):
        return pltpu.make_async_remote_copy(
            src_ref=keys_of(p, lane, i), dst_ref=PK.at[pl.ds(i * per_chunk, per_chunk)],
            send_sem=part_s.at[i], recv_sem=part_r.at[i],
            device_id=mirrored, device_id_type=MESH,
        )

    def copy_h(dr, dc):
        e = (dr + 1) * 3 + dc + 1
        if dc == 0:
            src = PQ.at[1 if dr < 0 else height, pl.ds(0, width)]
            dst = PQ.at[height + 1 if dr < 0 else 0, pl.ds(0, width)]
        else:
            side = 1 if dc > 0 else 0
            src, dst = CB.at[side], HB.at[1 - side, 1 - dr]
        return pltpu.make_async_remote_copy(
            src_ref=src, dst_ref=dst, send_sem=halo_s.at[e], recv_sem=halo_r.at[e],
            device_id=(r + dr, c + dc), device_id_type=MESH,
        )

    def hop(d, i):
        @pl.when(p - d >= 0)
        def _():
            q = p - d
            copy_z(q, i, True).wait_recv()
            pl.when(p < line - 1)(lambda: copy_z(q, i, True).start())
            copy_s(q, i, lane).start()

        @pl.when(p + d < line)
        def _():
            q = p + d
            copy_z(q, i, False).wait_recv()
            pl.when(p > 0)(lambda: copy_z(q, i, False).start())
            copy_s(q, i, lane).start()

    loads[0].wait()
    loads[1].wait()

    def step(k, carry):
        pltpu.make_async_copy(fk.at[pl.ds(0, CHUNK)], X.at[k], load.at[k]).wait()
        hidden = jnp.maximum(jnp.dot(X[k], WH[...], preferred_element_type=F32), 0.0)
        embedded = normalize(jnp.dot(hidden.astype(BF16), WO[...], preferred_element_type=F32))

        @pl.when(k < n_key)
        def _():
            KG[r, pl.ds(k * per_chunk, per_chunk)] = embedded.astype(BF16).reshape(per_chunk, BLOCK, -1)
            pl.when(p < line - 1)(lambda: copy_z(p, k, True).start())
            pl.when(p > 0)(lambda: copy_z(p, k, False).start())
            copy_s(p, k, lane).start()
            copy_p(k).start()

        @pl.when(k >= n_key)
        def _():
            first = (k - n_key) * img
            lines = embedded.reshape(img, width, -1)
            PQ[pl.ds(first + 1, img), pl.ds(0, width)] = lines.astype(BF16)
            for row in range(img):
                CF[0, pl.ds(first + row, 1)] = lines[row, 0:1]
                CF[1, pl.ds(first + row, 1)] = lines[row, width - 1 : width]

        for d in range(1, line):
            i = k - HOP_LAG * d
            pl.when((i >= 0) & (i < n_key))(functools.partial(hop, d, i))
        return carry

    lax.fori_loop(0, 2 * n_key, step, 0)

    CB[...] = CF[...].astype(BF16)
    for dr, dc in around:
        pl.when(inside(dr, dc))(lambda dr=dr, dc=dc: copy_h(dr, dc).start())
    for dr, dc in around:
        pl.when(inside(-dr, -dc))(lambda dr=dr, dc=dc: copy_h(dr, dc).wait_recv())

    halo = HB[...].astype(F32)
    place = lax.broadcasted_iota(jnp.int32, (pitch - width, halo.shape[-1]), 0)
    for b in range(height + 2):
        dr, row = (0, height - 1) if b == 0 else (2, 0) if b == height + 1 else (1, b - 1)
        left, right = halo[0, dr, row : row + 1], halo[1, dr, row : row + 1]
        both = jnp.where(place == 0, right, jnp.where(place == 1, left, 0.0))
        PQ[b, pl.ds(width, pitch - width)] = both.astype(BF16)

    def propagate(g, carry):
        own = PQ[pl.ds(g * GROUP + 1, GROUP), pl.ds(0, width)].reshape(GROUP * width, -1)
        beside = PQ[pl.ds(g * GROUP, GROUP + 2)].reshape(span, -1)
        weight = jnp.maximum(dot_t(own, beside), 0.0) * BAND[...]
        spread = dot_split(dot_split(weight * weight, beside), wp[...])
        blocks = GROUP * width // BLOCK
        PR[pl.ds(g * blocks, blocks)] = normalize(spread).astype(BF16).reshape(blocks, BLOCK, -1)
        return carry

    lax.fori_loop(0, height // GROUP, propagate, 0)

    for k in range(2 * n_key, n_key + HOP_LAG * (line - 1)):
        for d in range(1, line):
            if 0 <= k - HOP_LAG * d < n_key:
                hop(d, k - HOP_LAG * d)
    for i in range(n_key):
        copy_p(i).wait_recv()
        for q in range(line):
            copy_s(q, i, 1 - lane).wait_recv()

    key_px = lax.broadcasted_iota(jnp.int32, (BLOCK, BLOCK), 0)
    px = lax.broadcasted_iota(jnp.int32, (BLOCK, BLOCK), 1)
    line_of = px // width
    mirror = jnp.where(key_px == line_of * width + width - 1 - (px - line_of * width), INV_SHARP, 0.0).astype(F32)
    lines_per_block = BLOCK // width
    for b in range(per_tile):
        query = PR[b]
        total = jnp.zeros((1, BLOCK), F32)
        for n in range(shard.shape[-1]):
            negatives = KG[shard[0, 0, b, n], block[0, 0, b, n]]
            total += jnp.sum(jnp.exp(dot_t(negatives, query) * INV_SHARP), axis=0, keepdims=True)
        positive = jnp.sum(dot_t(PK[b], query) * mirror, axis=0, keepdims=True)
        loss = jnp.log(jnp.exp(positive) + total) - positive
        for row in range(lines_per_block):
            at = b * lines_per_block + row
            out[at : at + 1, :] = (
                valid[at : at + 1, :].astype(F32) * loss[:, row * width : (row + 1) * width]
            )

    for i in range(n_key):
        copy_p(i).wait_send()
    for dr, dc in around:
        pl.when(inside(dr, dc))(lambda dr=dr, dc=dc: copy_h(dr, dc).wait_send())

    def drain(q, carry):
        for i in range(n_key):
            copy_s(q, i, lane).wait_send()
            pl.when((q <= p) & (p < line - 1))(lambda i=i: copy_z(q, i, True).wait_send())
            pl.when((q >= p) & (p > 0))(lambda i=i: copy_z(q, i, False).wait_send())
        return carry

    lax.fori_loop(0, line, drain, 0)


def per_device(n_rows, n_cols, fq, fk, wh, wo, wp, valid, shard, block):
    height, width, channels = fq.shape
    pixels, wide, hid = height * width, wo.shape[1], wh.shape[1]
    n_key, per_tile, line = pixels // CHUNK, pixels // BLOCK, n_rows // 2
    pitch = width + 16
    any_space, vmem = pl.BlockSpec(memory_space=pl.ANY), pl.BlockSpec(memory_space=pltpu.VMEM)
    smem = pl.BlockSpec(memory_space=pltpu.SMEM)
    dma = pltpu.SemaphoreType.DMA
    return pl.pallas_call(
        functools.partial(kernel, n_rows, n_cols),
        out_shape=jax.ShapeDtypeStruct((height, width), F32),
        in_specs=[any_space] * 4 + [vmem, vmem, smem, smem],
        out_specs=vmem,
        scratch_shapes=[
            pltpu.VMEM((2 * n_key, CHUNK, channels), BF16),
            pltpu.VMEM((channels, hid), BF16),
            pltpu.VMEM((hid, wide), BF16),
            pltpu.VMEM((n_rows, per_tile, BLOCK, wide), BF16),
            pltpu.VMEM((per_tile, BLOCK, wide), BF16),
            pltpu.VMEM((height + 2, pitch, wide), BF16),
            pltpu.VMEM((2, height, wide), F32),
            pltpu.VMEM((2, height, wide), BF16),
            pltpu.VMEM((2, 3, height, wide), BF16),
            pltpu.VMEM((GROUP * width, (GROUP + 2) * pitch), F32),
            pltpu.VMEM((per_tile, BLOCK, wide), BF16),
            dma((2 * n_key,)),
            dma((2,)),
            dma((line, n_key)),
            dma((line, n_key)),
            dma((line, n_key)),
            dma((line, n_key)),
            dma((line, n_key)),
            dma((n_key,)),
            dma((n_key,)),
            dma((9,)),
            dma((9,)),
        ],
        compiler_params=pltpu.CompilerParams(
            collective_id=0, has_side_effects=True, vmem_limit_bytes=56 * 2**20
        ),
    )(fq.reshape(pixels, channels), fk.reshape(pixels, channels), wh, wo, wp, valid, shard, block)


def solution(mesh):
    tiles, heads = P("rows", "cols"), P("rows", "cols", None, None)
    return jax.shard_map(
        functools.partial(per_device, mesh.shape["rows"], mesh.shape["cols"]),
        mesh=mesh,
        in_specs=(P("rows", "cols", None), P("rows", "cols", None), P(), P(), P(), tiles, heads, heads),
        out_specs=tiles,
        check_vma=False,
    )
```

time: 87.1 us -> 59.1 us (0.68)
  the two profiles are of different devices: /device:TPU:18 before, /device:TPU:0 now
where the time goes in v1:
time: 59.1 us; the launch traced here: 58.8 us
  Pallas kernels  54.8 us (93%)
  local copies, waits for them, and re-layouts  3.98 us (7%)
    pallas_call x1, Pallas kernels, per_device(): pl.pallas_call(functools.partial(kernel, n_rows, n_cols), out_shape=jax.S...  54.8 us
    unnamed x3, local copies, waits for them, and re-layouts  3.98 us

profile of v1, /device:TPU:0, one launch (start us, length us, event | category | flops | bytes accessed | tf_op | source)
XLA Modules:
  0.0 58.8 jit_solution(957844321542673583)
XLA Ops:
  0.0 1.3 %copy.9.shard = s32[1,1,8,2]{3,2,1,0:T(8,128)} copy(s32[1,1,8,2]{2,3,1,0:T(2,128)} %param.14) | data formatting | bytes 128 | tf_op args[6]
  1.3 1.3 %copy.10.block = s32[1,1,8,2]{3,2,1,0:T(8,128)} copy(s32[1,1,8,2]{2,3,1,0:T(2,128)} %param.15) | data formatting | bytes 128 | tf_op args[7]
  2.7 54.8 %shard_map.82 = f32[16,64]{1,0:T(8,128)} custom-call(bf16[1024,2048]{1,0:T(8,128)(2,1)} %bitcast.2, bf16[1024,2048]{1,0:T(8,128)(2,1)} %bitcast.3, bf16[2048,2048]{1,0:T(8,128)(2,1)} %wh.1, bf16[2048,256]{1,0:T(8,128)(2,1)} %wo.1, bf16[256,256]{1,0:T(8,128)(2,1)} %wp.1, s32[16,64]{1,0:T(8,128)} %valid.1, s32[1,1,8,2]{3,2,1,0:T(8,128)} %copy.9.shard, ...), custom_call_target="tpu_custom_call" | custom-call | tf_op jit(solution)/shard_map/pallas_call | solution.py:261
  57.5 1.3 %copy.12 = f32[16,64]{1,0:T(8,128)} copy(f32[16,64]{1,0:T(8,128)} %shard_map.82) | data formatting | bytes 8192

commit v2 on v1

--- a/solution.py
+++ b/solution.py
@@ -10,7 +10,7 @@
 EPS = 1e-06
 INV_SHARP = 10.0
 CHUNK = 256
-HOP_LAG = 2
+HOP_LAG = 3
 GROUP = 4
 BLOCK = 128
 F32, BF16 = jnp.float32, jnp.bfloat16
@@ -224,8 +224,8 @@
     for b in range(per_tile):
         query = PR[b]
         total = jnp.zeros((1, BLOCK), F32)
-        for n in range(shard.shape[-1]):
-            negatives = KG[shard[0, 0, b, n], block[0, 0, b, n]]
+        for n in range(shard.shape[0]):
+            negatives = KG[shard[n, b], block[n, b]]
             total += jnp.sum(jnp.exp(dot_t(negatives, query) * INV_SHARP), axis=0, keepdims=True)
         positive = jnp.sum(dot_t(PK[b], query) * mirror, axis=0, keepdims=True)
         loss = jnp.log(jnp.exp(positive) + total) - positive
@@ -290,7 +290,7 @@
         compiler_params=pltpu.CompilerParams(
             collective_id=0, has_side_effects=True, vmem_limit_bytes=56 * 2**20
         ),
-    )(fq.reshape(pixels, channels), fk.reshape(pixels, channels), wh, wo, wp, valid, shard, block)
+    )(fq.reshape(pixels, channels), fk.reshape(pixels, channels), wh, wo, wp, valid, jnp.swapaxes(shard, 2, 3).reshape(-1, per_tile), jnp.swapaxes(block, 2, 3).reshape(-1, per_tile))
 
 
 def solution(mesh):

time: 59.1 us -> 52.5 us (0.89)
  Pallas kernels: 54.8 us -> 51 us
  local copies, waits for them, and re-layouts: 3.98 us -> 1.3 us
    pallas_call x1, Pallas kernels: 54.8 us -> 51 us  [per_device(): pl.pallas_call(functools.partial(kernel, n_rows, n_cols), out_shape=jax.S...]
    unnamed x3 -> x1, local copies, waits for them, and re-layouts: 3.98 us -> 1.3 us
where the time goes in v2:
time: 52.5 us; the launch traced here: 52.3 us
  Pallas kernels  51 us (97%)
  local copies, waits for them, and re-layouts  1.3 us (2%)
    pallas_call x1, Pallas kernels, per_device(): pl.pallas_call(functools.partial(kernel, n_rows, n_cols), out_shape=jax.S...  51 us
    unnamed x1, local copies, waits for them, and re-layouts  1.3 us

profile of v2, /device:TPU:0, one launch (start us, length us, event | category | flops | bytes accessed | tf_op | source)
XLA Modules:
  0.0 52.3 jit_solution(11680254355757532869)
XLA Ops:
  0.0 51.0 %shard_map.82 = f32[16,64]{1,0:T(8,128)} custom-call(bf16[1024,2048]{1,0:T(8,128)(2,1)} %bitcast.8, bf16[1024,2048]{1,0:T(8,128)(2,1)} %bitcast.9, bf16[2048,2048]{1,0:T(8,128)(2,1)} %wh.1, bf16[2048,256]{1,0:T(8,128)(2,1)} %wo.1, bf16[256,256]{1,0:T(8,128)(2,1)} %wp.1, s32[16,64]{1,0:T(8,128)} %valid.1, s32[2,8]{1,0:T(2,128)} %bitcast.10, s32[2,8]{1,0:T(2,128)} %bitcast.11), custom_call_target="tpu_custom_call" | custom-call | tf_op jit(solution)/shard_map/pallas_call | solution.py:261
  51.0 1.3 %copy.10 = f32[16,64]{1,0:T(8,128)} copy(f32[16,64]{1,0:T(8,128)} %shard_map.82) | data formatting | bytes 8192
